TPU v7x, 32 devices: a whole 2x2x4 slice. The times are simulated.
32 devices in a mesh: groups: 2 (over y), ctx: 4 (over z), head: 2 (over x), batch: 2 (over core).
Axes of the slice: x: 2, y: 2, z: 4, core: 2. Of those that a mesh axis runs over, the one named last changes fastest.
Arguments:
- queries: bfloat16 [4, 2048, 1024], P(('groups', 'batch'), 'ctx', 'head'), parts along dimension 0, may hold values from -200 to 200
- key_states: bfloat16 [4, 2048, 1024], P(('groups', 'batch'), 'ctx', 'head'), parts along dimension 0, may hold values from -16 to 16
- value_states: bfloat16 [4, 2048, 1024], P(('groups', 'batch'), 'ctx', 'head'), parts along dimension 0, may hold values from -16 to 16
- grad_out: bfloat16 [4, 2048, 1024], P(('groups', 'batch'), 'ctx'), parts along dimension 0, may hold values from -24 to 24
- out_weight: bfloat16 [1024, 1024], P('head'), may hold values from -0.1875 to 0.1875
Outputs:
- grad_queries: bfloat16 [4, 2048, 1024], P(('groups', 'batch'), 'ctx', 'head'), parts along dimension 0
- grad_keys: bfloat16 [4, 2048, 1024], P(('groups', 'batch'), 'ctx', 'head'), parts along dimension 0
- grad_values: bfloat16 [4, 2048, 1024], P(('groups', 'batch'), 'ctx', 'head'), parts along dimension 0
- grad_weight: float32 [2048, 1024], P(('groups', 'head')), parts along dimension 0
There are 2 independent parts, one for each index of `groups`. A program takes and returns all parts, laid end to end along the dimension named above; an argument that names none is the same for every part. Nothing has to cross between parts.
All inputs are finite; a program needn't handle non-finite values.
Results may differ from a plain program's by a relative error of at most 0.02.
Values may be sent and summed in bfloat16 or wider, within the bound.
A program may use at most 128 MiB of HBM per device.

v0:
```python
import functools
import math

import jax
import jax.numpy as jnp
from jax import lax
from jax.experimental import pallas as pl
from jax.experimental.pallas import tpu as pltpu
from jax.sharding import PartitionSpec as P

HD = 128
LEAF = 128
NEG_BIG = -1e30
F32 = jnp.float32
BF16 = jnp.bfloat16


def nn(a, b):
    return lax.dot_general(a, b, (((1,), (0,)), ((), ())), preferred_element_type=F32)


def nt(a, b):
    return lax.dot_general(a, b, (((1,), (1,)), ((), ())), preferred_element_type=F32)


def tn(a, b):
    return lax.dot_general(a, b, (((0,), (0,)), ((), ())), preferred_element_type=F32)


def pool_matrix(rows, entry):
    r = lax.broadcasted_iota(jnp.int32, (rows, 2 * rows), 0)
    c = lax.broadcasted_iota(jnp.int32, (rows, 2 * rows), 1)
    return jnp.where((c == 2 * r) | (c == 2 * r + 1), entry, 0.0).astype(BF16)


def spread_matrix(rows, entry):
    r = lax.broadcasted_iota(jnp.int32, (2 * rows, rows), 0)
    c = lax.broadcasted_iota(jnp.int32, (2 * rows, rows), 1)
    return jnp.where((r == 2 * c) | (r == 2 * c + 1), entry, 0.0).astype(BF16)


def kernel(
    n, heads, rows,
    q_ref, k_ref, v_ref, go_ref, w_ref,
    dq_ref, dk_ref, dv_ref, gw_ref,
    kp, kv1, kvl, ql, ga, sib, attn, e0, g0, d0, el, gl, dl, fal, fbl,
    xa, xb, xc, dkp, dkv1, gout, gin, rout, rin, dql,
    wpart, wsend, wrecv, wacc, wrs, wfin,
    halo_s, halo_r, sib_s, sib_r, gs_s, gs_r, rim_s, rim_r, wp_s, wp_r, rs_s, rs_r, ag_s, ag_r, wf_s, wf_r,
):
    MESH = pl.DeviceIdType.MESH
    ctx = lax.axis_index("ctx")
    core = lax.axis_index("batch")
    other = 1 - core
    cross = n.bit_length() - 1
    wide = heads * HD
    blocks = rows // LEAF
    local = blocks.bit_length() - 1
    levels = list(range(1, local + cross))
    top = levels[-1]
    scale = HD ** (-0.5)
    c2 = scale * math.log2(math.e)

    def at(l):
        return sum(rows >> i for i in range(1, l))

    barrier = pltpu.get_barrier_semaphore()
    for m in range(1, n):
        pl.semaphore_signal(barrier, inc=1, device_id={"ctx": ctx ^ m}, device_id_type=MESH)
    pl.semaphore_signal(barrier, inc=1, device_id={"batch": other}, device_id_type=MESH)

    kp[LEAF : LEAF + rows, :wide] = k_ref[...]
    kp[LEAF : LEAF + rows, wide:] = v_ref[...]

    half = pool_matrix(LEAF, 0.5)

    def pool(x, cnt):
        return nn(half[: cnt, : 2 * cnt], x).astype(BF16)

    for b in range(blocks // 2):
        kv1[b * LEAF : (b + 1) * LEAF] = pool(kp[LEAF + 2 * b * LEAF : LEAF + 2 * (b + 1) * LEAF], LEAF)
    kv2 = pool(kv1[...], LEAF)
    for b in range(cross):
        cnt = LEAF >> b
        kvl[b, :cnt] = kv2
        if b + 1 < cross:
            kv2 = pool(kv2, cnt // 2)

    @pl.when(ctx == 0)
    def _():
        kp[:LEAF] = jnp.zeros((LEAF, 2 * wide), BF16)

    @pl.when(ctx == n - 1)
    def _():
        kp[LEAF + rows :] = jnp.zeros((LEAF, 2 * wide), BF16)

    pl.semaphore_wait(barrier, n)

    def remote(src, dst, s, r, **dev):
        return pltpu.make_async_remote_copy(
            src_ref=src, dst_ref=dst, send_sem=s, recv_sem=r, device_id=dev, device_id_type=MESH
        )

    right = jnp.minimum(ctx + 1, n - 1)
    left = jnp.maximum(ctx - 1, 0)
    to_right = remote(kp.at[pl.ds(rows, LEAF)], kp.at[pl.ds(0, LEAF)], halo_s.at[0], halo_r.at[0], ctx=right)
    to_left = remote(kp.at[pl.ds(LEAF, LEAF)], kp.at[pl.ds(rows + LEAF, LEAF)], halo_s.at[1], halo_r.at[1], ctx=left)

    has_right = ctx < n - 1
    has_left = ctx > 0

    def run_if(cond, fn):
        @pl.when(cond)
        def _():
            fn()

    def sib_copies(b):
        cnt = LEAF >> b
        mine = lax.rem(ctx, 1 << b) * cnt
        out = []
        for j in range(1 << b):
            peer = ctx ^ ((1 << b) | j)
            slot = (1 << b) - 1 + j
            out.append(remote(
                kvl.at[b, pl.ds(0, cnt)], sib.at[b, pl.ds(pl.multiple_of(mine, cnt), cnt)],
                sib_s.at[slot], sib_r.at[slot], ctx=peer))
        return out

    def sib_arrivals(b):
        cnt = LEAF >> b
        out = []
        for j in range(1 << b):
            peer = ctx ^ ((1 << b) | j)
            slot = (1 << b) - 1 + j
            theirs = lax.rem(peer, 1 << b) * cnt
            out.append(remote(
                kvl.at[b, pl.ds(0, cnt)], sib.at[b, pl.ds(pl.multiple_of(theirs, cnt), cnt)],
                sib_s.at[slot], sib_r.at[slot], ctx=peer))
        return out

    run_if(has_right, to_right.start)
    run_if(has_left, to_left.start)
    for b in range(cross):
        for c in sib_copies(b):
            c.start()

    for b in range(blocks // 2):
        ql[b * LEAF : (b + 1) * LEAF] = pool(q_ref[2 * b * LEAF : 2 * (b + 1) * LEAF], LEAF)
    for l in levels[1:]:
        cnt = rows >> l
        ql[at(l) : at(l) + cnt] = pool(ql[at(l - 1) : at(l - 1) + 2 * cnt], cnt)
    for b in range(blocks):
        ga[b * LEAF : (b + 1) * LEAF] = nt(go_ref[b * LEAF : (b + 1) * LEAF], w_ref[...]).astype(BF16)

    def coarse_keys(l):
        if l < local:
            return [
                (c * LEAF, LEAF, kv1, (c ^ 1) * LEAF) for c in range((rows >> l) // LEAF)
            ]
        return [(0, rows >> l, sib.at[l - local], 0)]

    def wide_row(x, cnt):
        return jnp.broadcast_to(x, (cnt, HD))

    def spread(ref, x, cnt):
        ref[pl.ds(0, cnt, stride=2), :] = x
        ref[pl.ds(1, cnt, stride=2), :] = x
        return ref[pl.ds(0, 2 * cnt), :]

    def gather_pairs(ref, x, cnt):
        ref[pl.ds(0, 2 * cnt), :] = x
        return ref[pl.ds(0, cnt, stride=2), :] + ref[pl.ds(1, cnt, stride=2), :]

    run_if(has_left, to_right.wait_recv)
    run_if(has_right, to_left.wait_recv)
    for b in range(cross):
        for c in sib_arrivals(b):
            c.wait_recv()

    def forward(h, carry):
        hs = pl.ds(pl.multiple_of(h * HD, HD), HD)
        vs = pl.ds(pl.multiple_of(wide + h * HD, HD), HD)
        acc = None
        for l in reversed(levels):
            parts = []
            for r0, cnt, ref, k0 in coarse_keys(l):
                s = nt(ql[at(l) + r0 : at(l) + r0 + cnt, hs], ref[k0 : k0 + LEAF, hs]) * c2
                m = wide_row(jnp.max(s, axis=1, keepdims=True), cnt)
                e = jnp.exp2(s - m)
                eb = e.astype(BF16)
                el[h, at(l) + r0 : at(l) + r0 + cnt] = eb
                parts.append((m, wide_row(jnp.sum(e, axis=1, keepdims=True), cnt), nn(eb, ref[k0 : k0 + LEAF, vs])))
            m, s, o = [jnp.concatenate(x) if len(x) > 1 else x[0] for x in zip(*parts)]
            cnt = rows >> l
            if acc is None:
                acc = (m, s, o)
                fal[at(l) : at(l) + cnt] = jnp.ones((cnt, HD), F32)
            else:
                am, as_, ao = [spread(r, x, cnt // 2) for r, x in zip((xa, xb, xc), acc)]
                nm = jnp.maximum(m, am)
                fa = jnp.exp2(m - nm)
                fb = jnp.exp2(am - nm)
                fal[at(l) : at(l) + cnt] = fa
                fbl[at(l) : at(l) + cnt] = fb
                acc = (nm, fa * s + fb * as_, fa * o + fb * ao)
        am, as_, ao = [spread(r, x, rows // 2) for r, x in zip((xa, xb, xc), acc)]
        mixed = []
        for b in range(blocks):
            br = slice(b * LEAF, (b + 1) * LEAF)
            kr = slice(b * LEAF, (b + 3) * LEAF)
            s = nt(q_ref[br, hs], kp[kr, hs]) * c2
            if b == 0:
                col = lax.broadcasted_iota(jnp.int32, s.shape, 1)
                s = jnp.where((col >= LEAF) | has_left, s, NEG_BIG)
            if b == blocks - 1:
                col = lax.broadcasted_iota(jnp.int32, s.shape, 1)
                s = jnp.where((col < 2 * LEAF) | has_right, s, NEG_BIG)
            m = wide_row(jnp.max(s, axis=1, keepdims=True), LEAF)
            e = jnp.exp2(s - jnp.concatenate([m, m, m], axis=1))
            eb = e.astype(BF16)
            e0[h, br] = eb
            su = wide_row(jnp.sum(e, axis=1, keepdims=True), LEAF)
            o = nn(eb, kp[kr, vs])
            nm = jnp.maximum(m, am[br])
            fa = jnp.exp2(m - nm)
            fb = jnp.exp2(am[br] - nm)
            inv = 1.0 / (fa * su + fb * as_[br])
            at_b = ((fa * o + fb * ao[br]) * inv).astype(BF16)
            attn[br, hs] = at_b
            af = at_b.astype(F32)
            g = ga[br, hs].astype(F32)
            gb = (g * (fa * inv)).astype(BF16)
            g0[br, hs] = gb
            d0[h, br] = wide_row(jnp.sum(gb.astype(F32) * af, axis=1, keepdims=True), LEAF)
            r1 = fb * inv
            mixed.append((g * r1, r1 * wide_row(jnp.sum(g * af, axis=1, keepdims=True), LEAF)))
        gc = jnp.concatenate([x[0] for x in mixed])
        dc = jnp.concatenate([x[1] for x in mixed])
        for l in levels:
            cnt = rows >> l
            gc = gather_pairs(xa, gc, cnt)
            dc = gather_pairs(xb, dc, cnt)
            fa = fal[at(l) : at(l) + cnt]
            gl[h, at(l) : at(l) + cnt] = (gc * fa).astype(BF16)
            dl[h, at(l) : at(l) + cnt] = dc * fa
            if l != top:
                fb = fbl[at(l) : at(l) + cnt]
                gc = gc * fb
                dc = dc * fb
        return carry

    lax.fori_loop(0, heads, forward, 0)

    wrow = wide // 2
    piece = wrow // n
    for b in range(wide // LEAF):
        hb = slice(b * LEAF, (b + 1) * LEAF)
        wpart[hb] = tn(attn[:, hb], go_ref[...])
    wsend[...] = wpart[pl.ds(pl.multiple_of(other * wrow, wrow), wrow)].astype(BF16)
    wp = remote(wsend, wrecv, wp_s, wp_r, batch=other)
    wp.start()

    def coarse_back(h, l):
        hs = pl.ds(pl.multiple_of(h * HD, HD), HD)
        vs = pl.ds(pl.multiple_of(wide + h * HD, HD), HD)
        for r0, cnt, ref, k0 in coarse_keys(l):
            r = slice(at(l) + r0, at(l) + r0 + cnt)
            keys = ref[k0 : k0 + LEAF, hs]
            eb = el[h, r]
            g = gl[h, r]
            inner = nt(g, ref[k0 : k0 + LEAF, vs])
            ds = (eb.astype(F32) * (inner - dl[h, r])).astype(BF16)
            dql[r, hs] = nn(ds, keys) * scale
            dk = tn(ds, ql[r, hs]) * scale
            dv = tn(eb, g)
            if l < local:
                dkv1[k0 : k0 + LEAF, hs] = dk
                dkv1[k0 : k0 + LEAF, vs] = dv
            else:
                gout[l - local, :, hs] = dk.astype(BF16)
                gout[l - local, :, vs] = dv.astype(BF16)

    def back_cross(h, carry):
        for l in levels[local - 1 :]:
            coarse_back(h, l)
        return carry

    lax.fori_loop(0, heads, back_cross, 0)

    def grad_copies(b):
        cnt = LEAF >> b
        out = []
        for j in range(1 << b):
            peer = ctx ^ ((1 << b) | j)
            slot = (1 << b) - 1 + j
            theirs = lax.rem(peer, 1 << b) * cnt
            out.append(remote(
                gout.at[b, pl.ds(pl.multiple_of(theirs, cnt), cnt)], gin.at[slot, pl.ds(0, cnt)],
                gs_s.at[slot], gs_r.at[slot], ctx=peer))
        return out

    for b in range(cross):
        for c in grad_copies(b):
            c.start()

    wp.wait()
    my_rows = pl.multiple_of(core * wrow, wrow)
    wacc[...] = (wpart[pl.ds(my_rows, wrow)] + wrecv[...].astype(F32)).astype(BF16)
    rs = []
    for m in range(1, n):
        peer = ctx ^ m
        c = remote(
            wacc.at[pl.ds(pl.multiple_of(peer * piece, piece), piece)], wrs.at[m - 1],
            rs_s.at[m - 1], rs_r.at[m - 1], ctx=peer)
        c.start()
        rs.append(c)

    dkp[...] = jnp.zeros_like(dkp)

    def back_level0(h, carry):
        hs = pl.ds(pl.multiple_of(h * HD, HD), HD)
        vs = pl.ds(pl.multiple_of(wide + h * HD, HD), HD)
        for b in range(blocks):
            br = slice(b * LEAF, (b + 1) * LEAF)
            kr = slice(b * LEAF, (b + 3) * LEAF)
            eb = e0[h, br]
            gb = g0[br, hs]
            keys = kp[kr, hs]
            d = d0[h, br]
            inner = nt(gb, kp[kr, vs])
            ds = (eb.astype(F32) * (inner - jnp.concatenate([d, d, d], axis=1))).astype(BF16)
            xc[br] = nn(ds, keys) * scale
            dkp[kr, hs] += tn(ds, q_ref[br, hs]) * scale
            dkp[kr, vs] += tn(eb, gb)
        for l in levels[: local - 1]:
            coarse_back(h, l)
        chain = None
        for l in reversed(levels):
            cnt = rows >> l
            x = dql[at(l) : at(l) + cnt, hs]
            if chain is not None:
                x = x + spread(xa, chain * 0.5, cnt // 2)
            chain = x
        dq_ref[:, hs] = (xc[...] + spread(xa, chain * 0.5, rows // 2)).astype(BF16)
        return carry

    lax.fori_loop(0, heads, back_level0, 0)

    rout[0] = dkp[:LEAF].astype(BF16)
    rout[1] = dkp[LEAF + rows :].astype(BF16)
    rim_left = remote(rout.at[0], rin.at[1], rim_s.at[0], rim_r.at[1], ctx=left)
    rim_right = remote(rout.at[1], rin.at[0], rim_s.at[1], rim_r.at[0], ctx=right)
    run_if(has_left, rim_left.start)
    run_if(has_right, rim_right.start)

    for c in rs:
        c.wait()
    mine = pl.multiple_of(ctx * piece, piece)
    tot = wacc[pl.ds(mine, piece)].astype(F32)
    for m in range(1, n):
        tot = tot + wrs[m - 1].astype(F32)
    wfin[core, pl.ds(mine, piece)] = tot.astype(BF16)
    ags = []
    for m in range(1, n):
        peer = ctx ^ m
        c = remote(
            wfin.at[core, pl.ds(mine, piece)], wfin.at[core, pl.ds(mine, piece)],
            ag_s.at[m - 1], ag_r.at[m - 1], ctx=peer)
        c.start()
        ags.append(c)

    for b in range(cross):
        for c in grad_copies(b):
            c.wait()
    twice = spread_matrix(LEAF, 0.5)

    def spread_wide(x, cnt):
        return nn(twice[: 2 * cnt, : cnt], x.astype(BF16))

    chain = None
    for b in reversed(range(cross)):
        cnt = LEAF >> b
        x = 0.0
        for j in range(1 << b):
            x = x + gin[(1 << b) - 1 + j, :cnt].astype(F32)
        if chain is not None:
            x = x + spread_wide(chain, cnt // 2)
        chain = x
    dkv1[...] += spread_wide(chain, LEAF)
    for b in range(blocks // 2):
        dkp[LEAF * (1 + 2 * b) : LEAF * (3 + 2 * b)] += spread_wide(dkv1[b * LEAF : (b + 1) * LEAF], LEAF)

    def left_arrival():
        rim_right.wait_recv()
        dkp[LEAF : 2 * LEAF] += rin[0].astype(F32)

    def right_arrival():
        rim_left.wait_recv()
        dkp[rows : rows + LEAF] += rin[1].astype(F32)

    run_if(has_left, left_arrival)
    run_if(has_right, right_arrival)
    dk_ref[...] = dkp[LEAF : LEAF + rows, :wide].astype(BF16)
    dv_ref[...] = dkp[LEAF : LEAF + rows, wide:].astype(BF16)

    for m in range(1, n):
        peer = ctx ^ m
        theirs = pl.multiple_of(peer * piece, piece)
        remote(
            wfin.at[core, pl.ds(mine, piece)], wfin.at[core, pl.ds(theirs, piece)],
            ag_s.at[m - 1], ag_r.at[m - 1], ctx=peer).wait_recv()
    for c in ags:
        c.wait_send()
    wf = remote(wfin.at[core], wfin.at[core], wf_s, wf_r, batch=other)
    wf.start()
    gw_ref[pl.ds(my_rows, wrow)] = wfin[core].astype(F32)
    remote(wfin.at[core], wfin.at[other], wf_s, wf_r, batch=other).wait_recv()
    gw_ref[pl.ds(pl.multiple_of(other * wrow, wrow), wrow)] = wfin[other].astype(F32)
    wf.wait_send()

    run_if(has_right, to_right.wait_send)
    run_if(has_left, to_left.wait_send)
    for b in range(cross):
        for c in sib_copies(b):
            c.wait_send()
    run_if(has_left, rim_left.wait_send)
    run_if(has_right, rim_right.wait_send)


def body(queries, key_states, value_states, grad_out, out_weight):
    n = lax.axis_size("ctx")
    rows, wide = queries.shape[1:]
    heads = wide // HD
    cross = n.bit_length() - 1
    width = grad_out.shape[2]
    coarse = sum(rows >> l for l in range(1, (rows // LEAF).bit_length() - 1 + cross))
    wrow = wide // 2
    piece = wrow // n
    pieces = n - 1
    vm = pltpu.VMEM
    dma = pltpu.SemaphoreType.DMA
    scratch = [
        vm((rows + 2 * LEAF, 2 * wide), BF16),
        vm((rows // 2, 2 * wide), BF16),
        vm((cross, LEAF, 2 * wide), BF16),
        vm((coarse, wide), BF16),
        vm((rows, wide), BF16),
        vm((cross, LEAF, 2 * wide), BF16),
        vm((rows, wide), BF16),
        vm((heads, rows, 3 * LEAF), BF16),
        vm((rows, wide), BF16),
        vm((heads, rows, HD), F32),
        vm((heads, coarse, LEAF), BF16),
        vm((heads, coarse, HD), BF16),
        vm((heads, coarse, HD), F32),
        vm((coarse, HD), F32),
        vm((coarse, HD), F32),
        vm((rows, HD), F32),
        vm((rows, HD), F32),
        vm((rows, HD), F32),
        vm((rows + 2 * LEAF, 2 * wide), F32),
        vm((rows // 2, 2 * wide), F32),
        vm((cross, LEAF, 2 * wide), BF16),
        vm((pieces, LEAF, 2 * wide), BF16),
        vm((2, LEAF, 2 * wide), BF16),
        vm((2, LEAF, 2 * wide), BF16),
        vm((coarse, wide), F32),
        vm((wide, width), F32),
        vm((wrow, width), BF16),
        vm((wrow, width), BF16),
        vm((wrow, width), BF16),
        vm((pieces, piece, width), BF16),
        vm((2, wrow, width), BF16),
        dma((2,)), dma((2,)),
        dma((pieces,)), dma((pieces,)),
        dma((pieces,)), dma((pieces,)),
        dma((2,)), dma((2,)),
        dma, dma,
        dma((pieces,)), dma((pieces,)),
        dma((pieces,)), dma((pieces,)),
        dma, dma,
    ]
    spec = pl.BlockSpec(memory_space=pltpu.VMEM)
    out = pl.pallas_call(
        functools.partial(kernel, n, heads, rows),
        out_shape=[jax.ShapeDtypeStruct((rows, wide), BF16)] * 3
        + [jax.ShapeDtypeStruct((wide, width), F32)],
        in_specs=[spec] * 5,
        out_specs=[spec] * 4,
        scratch_shapes=scratch,
        compiler_params=pltpu.CompilerParams(
            collective_id=0, has_side_effects=True, vmem_limit_bytes=56 * 2**20
        ),
    )(queries[0], key_states[0], value_states[0], grad_out[0], out_weight)
    return out[0][None], out[1][None], out[2][None], out[3]


def solution(mesh):
    row = P(("groups", "batch"), "ctx", "head")
    in_specs = (row, row, row, P(("groups", "batch"), "ctx", None), P("head", None))
    out_specs = (row, row, row, P(("groups", "head"), None))
    return jax.shard_map(body, mesh=mesh, in_specs=in_specs, out_specs=out_specs, check_vma=False)
```

profile of v0, /device:TPU:0, one launch (start us, length us, event | category | flops | bytes accessed | tf_op | source)
XLA Modules:
  0.0 86.7 jit_solution(6448074023305037696)
XLA Ops:
  0.6 79.0 %shard_map.84 = (bf16[512,512]{1,0:T(8,128)(2,1)}, bf16[512,512]{1,0:T(8,128)(2,1)}, bf16[512,512]{1,0:T(8,128)(2,1)}, f32[512,1024]{1,0:T(8,128)}) custom-call(bf16[512,512]{1,0:T(8,128)(2,1)} %bitcast.8, bf16[512,512]{1,0:T(8,128)(2,1)} %bitcast.9, bf16[512,512]{1,0:T(8,128)(2,1)} %bitcast.10, bf16[512,1024]{1,0:T(8,128)(2,1)} %bitcast.7, ...), custom_call_target="tpu_custom_call" | custom-call | tf_op jit(solution)/shard_map/pallas_call | solution.py:484
  79.7 0.0 copy-start
  79.7 2.0 %copy.13 = bf16[1,512,512]{2,1,0:T(8,128)(2,1)} copy(bf16[1,512,512]{2,1,0:T(8,128)(2,1)} %bitcast.13) | data formatting | bytes 1048576
  81.7 1.9 %copy.14 = bf16[1,512,512]{2,1,0:T(8,128)(2,1)} copy(bf16[1,512,512]{2,1,0:T(8,128)(2,1)} %bitcast.12) | data formatting | bytes 1048576
  83.5 1.9 %copy.15 = bf16[1,512,512]{2,1,0:T(8,128)(2,1)} copy(bf16[1,512,512]{2,1,0:T(8,128)(2,1)} %bitcast.11) | data formatting | bytes 1048576
  85.4 0.0 copy-done
  85.4 1.3 %copy.16 = f32[512,1024]{1,0:T(8,128)} copy(f32[512,1024]{1,0:T(8,128)S(1)} %copy-done) | data formatting | bytes 4194304
Async XLA Ops:
  79.7 5.8 %copy-start = (f32[512,1024]{1,0:T(8,128)S(1)}, f32[512,1024]{1,0:T(8,128)}, u32[]{:S(2)}) copy-start(f32[512,1024]{1,0:T(8,128)} %get-tuple-element.19) | copy-start | bytes 6291460
where the time goes:
time: 87 us; the launch traced here: 86.7 us
  Pallas kernels  79 us (91%)
  local copies, waits for them, and re-layouts  7.07 us (8%)
    pallas_call x1, Pallas kernels, body(): pl.pallas_call(functools.partial(kernel, n, heads, rows), out_shape=[jax....  79 us
    unnamed x6, local copies, waits for them, and re-layouts  7.07 us

commit v1 on v0

--- a/solution.py
+++ b/solution.py
@@ -40,12 +40,12 @@
 
 
 def kernel(
-    n, heads, rows,
+    n, heads, rows, halves,
     q_ref, k_ref, v_ref, go_ref, w_ref,
-    dq_ref, dk_ref, dv_ref, gw_ref,
+    dq_ref, dk_ref, dv_ref, wf_ref,
     kp, kv1, kvl, ql, ga, sib, attn, e0, g0, d0, el, gl, dl, fal, fbl,
     xa, xb, xc, dkp, dkv1, gout, gin, rout, rin, dql,
-    wpart, wsend, wrecv, wacc, wrs, wfin,
+    wpart, wsend, wrecv, wacc, wtx, wrx, wfin,
     halo_s, halo_r, sib_s, sib_r, gs_s, gs_r, rim_s, rim_r, wp_s, wp_r, rs_s, rs_r, ag_s, ag_r, wf_s, wf_r,
 ):
     MESH = pl.DeviceIdType.MESH
@@ -69,8 +69,21 @@
         pl.semaphore_signal(barrier, inc=1, device_id={"ctx": ctx ^ m}, device_id_type=MESH)
     pl.semaphore_signal(barrier, inc=1, device_id={"batch": other}, device_id_type=MESH)
 
-    kp[LEAF : LEAF + rows, :wide] = k_ref[...]
-    kp[LEAF : LEAF + rows, wide:] = v_ref[...]
+    per = heads // halves
+    hw = per * HD
+
+    def kcol(h):
+        return pl.ds(pl.multiple_of((h // per) * 2 * hw + lax.rem(h, per) * HD, HD), HD)
+
+    def vcol(h):
+        return pl.ds(pl.multiple_of((h // per) * 2 * hw + hw + lax.rem(h, per) * HD, HD), HD)
+
+    def hcol(u):
+        return pl.ds(u * 2 * hw, 2 * hw)
+
+    for u in range(halves):
+        kp[LEAF : LEAF + rows, u * 2 * hw : u * 2 * hw + hw] = k_ref[:, u * hw : (u + 1) * hw]
+        kp[LEAF : LEAF + rows, u * 2 * hw + hw : (u + 1) * 2 * hw] = v_ref[:, u * hw : (u + 1) * hw]
 
     half = pool_matrix(LEAF, 0.5)
 
@@ -103,8 +116,14 @@
 
     right = jnp.minimum(ctx + 1, n - 1)
     left = jnp.maximum(ctx - 1, 0)
-    to_right = remote(kp.at[pl.ds(rows, LEAF)], kp.at[pl.ds(0, LEAF)], halo_s.at[0], halo_r.at[0], ctx=right)
-    to_left = remote(kp.at[pl.ds(LEAF, LEAF)], kp.at[pl.ds(rows + LEAF, LEAF)], halo_s.at[1], halo_r.at[1], ctx=left)
+
+    def to_right(u):
+        return remote(kp.at[pl.ds(rows, LEAF), hcol(u)], kp.at[pl.ds(0, LEAF), hcol(u)],
+                      halo_s.at[u, 0], halo_r.at[u, 0], ctx=right)
+
+    def to_left(u):
+        return remote(kp.at[pl.ds(LEAF, LEAF), hcol(u)], kp.at[pl.ds(rows + LEAF, LEAF), hcol(u)],
+                      halo_s.at[u, 1], halo_r.at[u, 1], ctx=left)
 
     has_right = ctx < n - 1
     has_left = ctx > 0
@@ -114,7 +133,7 @@
         def _():
             fn()
 
-    def sib_copies(b):
+    def sib_copies(u, b):
         cnt = LEAF >> b
         mine = lax.rem(ctx, 1 << b) * cnt
         out = []
@@ -122,11 +141,11 @@
             peer = ctx ^ ((1 << b) | j)
             slot = (1 << b) - 1 + j
             out.append(remote(
-                kvl.at[b, pl.ds(0, cnt)], sib.at[b, pl.ds(pl.multiple_of(mine, cnt), cnt)],
-                sib_s.at[slot], sib_r.at[slot], ctx=peer))
+                kvl.at[b, pl.ds(0, cnt), hcol(u)], sib.at[b, pl.ds(pl.multiple_of(mine, cnt), cnt), hcol(u)],
+                sib_s.at[u, slot], sib_r.at[u, slot], ctx=peer))
         return out
 
-    def sib_arrivals(b):
+    def sib_arrivals(u, b):
         cnt = LEAF >> b
         out = []
         for j in range(1 << b):
@@ -134,15 +153,32 @@
             slot = (1 << b) - 1 + j
             theirs = lax.rem(peer, 1 << b) * cnt
             out.append(remote(
-                kvl.at[b, pl.ds(0, cnt)], sib.at[b, pl.ds(pl.multiple_of(theirs, cnt), cnt)],
-                sib_s.at[slot], sib_r.at[slot], ctx=peer))
+                kvl.at[b, pl.ds(0, cnt), hcol(u)], sib.at[b, pl.ds(pl.multiple_of(theirs, cnt), cnt), hcol(u)],
+                sib_s.at[u, slot], sib_r.at[u, slot], ctx=peer))
         return out
 
-    run_if(has_right, to_right.start)
-    run_if(has_left, to_left.start)
-    for b in range(cross):
-        for c in sib_copies(b):
-            c.start()
+    def send_kv(u):
+        run_if(has_right, to_right(u).start)
+        run_if(has_left, to_left(u).start)
+        for b in range(cross):
+            for c in sib_copies(u, b):
+                c.start()
+
+    def take_kv(u):
+        run_if(has_left, to_right(u).wait_recv)
+        run_if(has_right, to_left(u).wait_recv)
+        for b in range(cross):
+            for c in sib_arrivals(u, b):
+                c.wait_recv()
+
+    def sent_kv(u):
+        run_if(has_right, to_right(u).wait_send)
+        run_if(has_left, to_left(u).wait_send)
+        for b in range(cross):
+            for c in sib_copies(u, b):
+                c.wait_send()
+
+    send_kv(0)
 
     for b in range(blocks // 2):
         ql[b * LEAF : (b + 1) * LEAF] = pool(q_ref[2 * b * LEAF : 2 * (b + 1) * LEAF], LEAF)
@@ -171,20 +207,15 @@
         ref[pl.ds(0, 2 * cnt), :] = x
         return ref[pl.ds(0, cnt, stride=2), :] + ref[pl.ds(1, cnt, stride=2), :]
 
-    run_if(has_left, to_right.wait_recv)
-    run_if(has_right, to_left.wait_recv)
-    for b in range(cross):
-        for c in sib_arrivals(b):
-            c.wait_recv()
-
     def forward(h, carry):
         hs = pl.ds(pl.multiple_of(h * HD, HD), HD)
-        vs = pl.ds(pl.multiple_of(wide + h * HD, HD), HD)
+        ks = kcol(h)
+        vs = vcol(h)
         acc = None
         for l in reversed(levels):
             parts = []
             for r0, cnt, ref, k0 in coarse_keys(l):
-                s = nt(ql[at(l) + r0 : at(l) + r0 + cnt, hs], ref[k0 : k0 + LEAF, hs]) * c2
+                s = nt(ql[at(l) + r0 : at(l) + r0 + cnt, hs], ref[k0 : k0 + LEAF, ks]) * c2
                 m = wide_row(jnp.max(s, axis=1, keepdims=True), cnt)
                 e = jnp.exp2(s - m)
                 eb = e.astype(BF16)
@@ -208,7 +239,7 @@
         for b in range(blocks):
             br = slice(b * LEAF, (b + 1) * LEAF)
             kr = slice(b * LEAF, (b + 3) * LEAF)
-            s = nt(q_ref[br, hs], kp[kr, hs]) * c2
+            s = nt(q_ref[br, hs], kp[kr, ks]) * c2
             if b == 0:
                 col = lax.broadcasted_iota(jnp.int32, s.shape, 1)
                 s = jnp.where((col >= LEAF) | has_left, s, NEG_BIG)
@@ -249,23 +280,62 @@
                 dc = dc * fb
         return carry
 
-    lax.fori_loop(0, heads, forward, 0)
-
-    wrow = wide // 2
-    piece = wrow // n
-    for b in range(wide // LEAF):
-        hb = slice(b * LEAF, (b + 1) * LEAF)
-        wpart[hb] = tn(attn[:, hb], go_ref[...])
-    wsend[...] = wpart[pl.ds(pl.multiple_of(other * wrow, wrow), wrow)].astype(BF16)
-    wp = remote(wsend, wrecv, wp_s, wp_r, batch=other)
-    wp.start()
+    half_cols = go_ref.shape[1] // 2
+    steps = cross
+    my_cols = pl.ds(pl.multiple_of(core * half_cols, half_cols), half_cols)
+    other_cols = pl.ds(pl.multiple_of(other * half_cols, half_cols), half_cols)
+
+    def bit(s):
+        return lax.rem(ctx // (1 << s), 2)
+
+    def weight_grad(u):
+        for b in range(per):
+            wpart[u, b * HD : (b + 1) * HD] = tn(attn[:, u * hw + b * HD : u * hw + (b + 1) * HD], go_ref[...])
+        wsend[u] = wpart[u, :, other_cols].astype(BF16)
+        pair = remote(wsend.at[u], wrecv.at[u], wp_s.at[u], wp_r.at[u], batch=other)
+        pair.start()
+        yield
+        pair.wait()
+        wacc[u] = wpart[u, :, my_cols] + wrecv[u].astype(F32)
+        lo, size, got = 0, hw, 0
+        for s in range(steps):
+            size //= 2
+            give = pl.multiple_of(lo + (1 - bit(s)) * size, size)
+            lo = lo + bit(s) * size
+            keep = pl.multiple_of(lo, size)
+            wtx[u, pl.ds(give, size)] = wacc[u, pl.ds(give, size)].astype(BF16)
+            c = remote(wtx.at[u, pl.ds(give, size)], wrx.at[u, pl.ds(got, size)],
+                       rs_s.at[u, s], rs_r.at[u, s], ctx=ctx ^ (1 << s))
+            c.start()
+            yield
+            c.wait()
+            wacc[u, pl.ds(keep, size)] += wrx[u, pl.ds(got, size)].astype(F32)
+            got += size
+        wfin[u, core, pl.ds(pl.multiple_of(lo, size), size)] = wacc[u, pl.ds(pl.multiple_of(lo, size), size)].astype(BF16)
+        for s in reversed(range(steps)):
+            mine = pl.ds(pl.multiple_of(lo, size), size)
+            theirs = pl.ds(pl.multiple_of(lo + (1 - 2 * bit(s)) * size, size), size)
+            peer = ctx ^ (1 << s)
+            c = remote(wfin.at[u, core, mine], wfin.at[u, core, mine], ag_s.at[u, s], ag_r.at[u, s], ctx=peer)
+            c.start()
+            yield
+            c.wait_send()
+            remote(wfin.at[u, core, mine], wfin.at[u, core, theirs], ag_s.at[u, s], ag_r.at[u, s], ctx=peer).wait_recv()
+            lo = lo - bit(s) * size
+            size *= 2
+        c = remote(wfin.at[u, core], wfin.at[u, core], wf_s.at[u], wf_r.at[u], batch=other)
+        c.start()
+        yield
+        c.wait_send()
+        remote(wfin.at[u, core], wfin.at[u, other], wf_s.at[u], wf_r.at[u], batch=other).wait_recv()
 
     def coarse_back(h, l):
         hs = pl.ds(pl.multiple_of(h * HD, HD), HD)
-        vs = pl.ds(pl.multiple_of(wide + h * HD, HD), HD)
+        ks = kcol(h)
+        vs = vcol(h)
         for r0, cnt, ref, k0 in coarse_keys(l):
             r = slice(at(l) + r0, at(l) + r0 + cnt)
-            keys = ref[k0 : k0 + LEAF, hs]
+            keys = ref[k0 : k0 + LEAF, ks]
             eb = el[h, r]
             g = gl[h, r]
             inner = nt(g, ref[k0 : k0 + LEAF, vs])
@@ -274,10 +344,10 @@
             dk = tn(ds, ql[r, hs]) * scale
             dv = tn(eb, g)
             if l < local:
-                dkv1[k0 : k0 + LEAF, hs] = dk
+                dkv1[k0 : k0 + LEAF, ks] = dk
                 dkv1[k0 : k0 + LEAF, vs] = dv
             else:
-                gout[l - local, :, hs] = dk.astype(BF16)
+                gout[l - local, :, ks] = dk.astype(BF16)
                 gout[l - local, :, vs] = dv.astype(BF16)
 
     def back_cross(h, carry):
@@ -285,9 +355,7 @@
             coarse_back(h, l)
         return carry
 
-    lax.fori_loop(0, heads, back_cross, 0)
-
-    def grad_copies(b):
+    def grad_copies(u, b):
         cnt = LEAF >> b
         out = []
         for j in range(1 << b):
@@ -295,42 +363,27 @@
             slot = (1 << b) - 1 + j
             theirs = lax.rem(peer, 1 << b) * cnt
             out.append(remote(
-                gout.at[b, pl.ds(pl.multiple_of(theirs, cnt), cnt)], gin.at[slot, pl.ds(0, cnt)],
-                gs_s.at[slot], gs_r.at[slot], ctx=peer))
+                gout.at[b, pl.ds(pl.multiple_of(theirs, cnt), cnt), hcol(u)], gin.at[slot, pl.ds(0, cnt), hcol(u)],
+                gs_s.at[u, slot], gs_r.at[u, slot], ctx=peer))
         return out
-
-    for b in range(cross):
-        for c in grad_copies(b):
-            c.start()
-
-    wp.wait()
-    my_rows = pl.multiple_of(core * wrow, wrow)
-    wacc[...] = (wpart[pl.ds(my_rows, wrow)] + wrecv[...].astype(F32)).astype(BF16)
-    rs = []
-    for m in range(1, n):
-        peer = ctx ^ m
-        c = remote(
-            wacc.at[pl.ds(pl.multiple_of(peer * piece, piece), piece)], wrs.at[m - 1],
-            rs_s.at[m - 1], rs_r.at[m - 1], ctx=peer)
-        c.start()
-        rs.append(c)
 
     dkp[...] = jnp.zeros_like(dkp)
 
     def back_level0(h, carry):
         hs = pl.ds(pl.multiple_of(h * HD, HD), HD)
-        vs = pl.ds(pl.multiple_of(wide + h * HD, HD), HD)
+        ks = kcol(h)
+        vs = vcol(h)
         for b in range(blocks):
             br = slice(b * LEAF, (b + 1) * LEAF)
             kr = slice(b * LEAF, (b + 3) * LEAF)
             eb = e0[h, br]
             gb = g0[br, hs]
-            keys = kp[kr, hs]
+            keys = kp[kr, ks]
             d = d0[h, br]
             inner = nt(gb, kp[kr, vs])
             ds = (eb.astype(F32) * (inner - jnp.concatenate([d, d, d], axis=1))).astype(BF16)
             xc[br] = nn(ds, keys) * scale
-            dkp[kr, hs] += tn(ds, q_ref[br, hs]) * scale
+            dkp[kr, ks] += tn(ds, q_ref[br, hs]) * scale
             dkp[kr, vs] += tn(eb, gb)
         for l in levels[: local - 1]:
             coarse_back(h, l)
@@ -344,87 +397,99 @@
         dq_ref[:, hs] = (xc[...] + spread(xa, chain * 0.5, rows // 2)).astype(BF16)
         return carry
 
-    lax.fori_loop(0, heads, back_level0, 0)
-
-    rout[0] = dkp[:LEAF].astype(BF16)
-    rout[1] = dkp[LEAF + rows :].astype(BF16)
-    rim_left = remote(rout.at[0], rin.at[1], rim_s.at[0], rim_r.at[1], ctx=left)
-    rim_right = remote(rout.at[1], rin.at[0], rim_s.at[1], rim_r.at[0], ctx=right)
-    run_if(has_left, rim_left.start)
-    run_if(has_right, rim_right.start)
-
-    for c in rs:
-        c.wait()
-    mine = pl.multiple_of(ctx * piece, piece)
-    tot = wacc[pl.ds(mine, piece)].astype(F32)
-    for m in range(1, n):
-        tot = tot + wrs[m - 1].astype(F32)
-    wfin[core, pl.ds(mine, piece)] = tot.astype(BF16)
-    ags = []
-    for m in range(1, n):
-        peer = ctx ^ m
-        c = remote(
-            wfin.at[core, pl.ds(mine, piece)], wfin.at[core, pl.ds(mine, piece)],
-            ag_s.at[m - 1], ag_r.at[m - 1], ctx=peer)
-        c.start()
-        ags.append(c)
-
-    for b in range(cross):
-        for c in grad_copies(b):
-            c.wait()
+    def rim_left(u):
+        return remote(rout.at[0, :, hcol(u)], rin.at[1, :, hcol(u)], rim_s.at[u, 0], rim_r.at[u, 1], ctx=left)
+
+    def rim_right(u):
+        return remote(rout.at[1, :, hcol(u)], rin.at[0, :, hcol(u)], rim_s.at[u, 1], rim_r.at[u, 0], ctx=right)
+
     twice = spread_matrix(LEAF, 0.5)
 
     def spread_wide(x, cnt):
         return nn(twice[: 2 * cnt, : cnt], x.astype(BF16))
 
-    chain = None
-    for b in reversed(range(cross)):
-        cnt = LEAF >> b
-        x = 0.0
-        for j in range(1 << b):
-            x = x + gin[(1 << b) - 1 + j, :cnt].astype(F32)
-        if chain is not None:
-            x = x + spread_wide(chain, cnt // 2)
-        chain = x
-    dkv1[...] += spread_wide(chain, LEAF)
-    for b in range(blocks // 2):
-        dkp[LEAF * (1 + 2 * b) : LEAF * (3 + 2 * b)] += spread_wide(dkv1[b * LEAF : (b + 1) * LEAF], LEAF)
-
-    def left_arrival():
-        rim_right.wait_recv()
-        dkp[LEAF : 2 * LEAF] += rin[0].astype(F32)
-
-    def right_arrival():
-        rim_left.wait_recv()
-        dkp[rows : rows + LEAF] += rin[1].astype(F32)
-
-    run_if(has_left, left_arrival)
-    run_if(has_right, right_arrival)
-    dk_ref[...] = dkp[LEAF : LEAF + rows, :wide].astype(BF16)
-    dv_ref[...] = dkp[LEAF : LEAF + rows, wide:].astype(BF16)
-
-    for m in range(1, n):
-        peer = ctx ^ m
-        theirs = pl.multiple_of(peer * piece, piece)
-        remote(
-            wfin.at[core, pl.ds(mine, piece)], wfin.at[core, pl.ds(theirs, piece)],
-            ag_s.at[m - 1], ag_r.at[m - 1], ctx=peer).wait_recv()
-    for c in ags:
-        c.wait_send()
-    wf = remote(wfin.at[core], wfin.at[core], wf_s, wf_r, batch=other)
-    wf.start()
-    gw_ref[pl.ds(my_rows, wrow)] = wfin[core].astype(F32)
-    remote(wfin.at[core], wfin.at[other], wf_s, wf_r, batch=other).wait_recv()
-    gw_ref[pl.ds(pl.multiple_of(other * wrow, wrow), wrow)] = wfin[other].astype(F32)
-    wf.wait_send()
-
-    run_if(has_right, to_right.wait_send)
-    run_if(has_left, to_left.wait_send)
-    for b in range(cross):
-        for c in sib_copies(b):
-            c.wait_send()
-    run_if(has_left, rim_left.wait_send)
-    run_if(has_right, rim_right.wait_send)
+    def send_grads(u):
+        for b in range(cross):
+            for c in grad_copies(u, b):
+                c.start()
+
+    def send_rims(u):
+        rout[0, :, hcol(u)] = dkp[:LEAF, hcol(u)].astype(BF16)
+        rout[1, :, hcol(u)] = dkp[LEAF + rows :, hcol(u)].astype(BF16)
+        run_if(has_left, rim_left(u).start)
+        run_if(has_right, rim_right(u).start)
+
+    def finish(u):
+        for b in range(cross):
+            for c in grad_copies(u, b):
+                c.wait()
+        chain = None
+        for b in reversed(range(cross)):
+            cnt = LEAF >> b
+            x = 0.0
+            for j in range(1 << b):
+                x = x + gin[(1 << b) - 1 + j, :cnt, hcol(u)].astype(F32)
+            if chain is not None:
+                x = x + spread_wide(chain, cnt // 2)
+            chain = x
+        dkv1[:, hcol(u)] += spread_wide(chain, LEAF)
+        for b in range(blocks // 2):
+            dkp[LEAF * (1 + 2 * b) : LEAF * (3 + 2 * b), hcol(u)] += spread_wide(
+                dkv1[b * LEAF : (b + 1) * LEAF, hcol(u)], LEAF)
+
+        def left_arrival():
+            rim_right(u).wait_recv()
+            dkp[LEAF : 2 * LEAF, hcol(u)] += rin[0, :, hcol(u)].astype(F32)
+
+        def right_arrival():
+            rim_left(u).wait_recv()
+            dkp[rows : rows + LEAF, hcol(u)] += rin[1, :, hcol(u)].astype(F32)
+
+        run_if(has_left, left_arrival)
+        run_if(has_right, right_arrival)
+        dk_ref[:, u * hw : (u + 1) * hw] = dkp[LEAF : LEAF + rows, u * 2 * hw : u * 2 * hw + hw].astype(BF16)
+        dv_ref[:, u * hw : (u + 1) * hw] = dkp[LEAF : LEAF + rows, u * 2 * hw + hw : (u + 1) * 2 * hw].astype(BF16)
+
+    chains = []
+
+    def advance():
+        for c in list(chains):
+            if next(c, chains) is chains:
+                chains.remove(c)
+
+    for u in range(halves):
+        take_kv(u)
+        if u + 1 < halves:
+            send_kv(u + 1)
+        lax.fori_loop(u * per, (u + 1) * per, forward, 0)
+        chains.append(weight_grad(u))
+        advance()
+        lax.fori_loop(u * per, (u + 1) * per, back_cross, 0)
+        send_grads(u)
+        advance()
+        lax.fori_loop(u * per, (u + 1) * per, back_level0, 0)
+        send_rims(u)
+        advance()
+    for u in range(halves):
+        finish(u)
+        advance()
+    while chains:
+        advance()
+    wf_ref[...] = wfin[...]
+    for u in range(halves):
+        sent_kv(u)
+        run_if(has_left, rim_left(u).wait_send)
+        run_if(has_right, rim_right(u).wait_send)
+
+
+def settle(dq_in, dk_in, dv_in, wf, dq, dk, dv, gw):
+    dq[...] = dq_in[...]
+    dk[...] = dk_in[...]
+    dv[...] = dv_in[...]
+    halves, cores, size, cols = wf.shape
+    for u in range(halves):
+        for c in range(cores):
+            gw[u * size : (u + 1) * size, c * cols : (c + 1) * cols] = wf[u, c].astype(F32)
 
 
 def body(queries, key_states, value_states, grad_out, out_weight):
@@ -434,8 +499,9 @@
     cross = n.bit_length() - 1
     width = grad_out.shape[2]
     coarse = sum(rows >> l for l in range(1, (rows // LEAF).bit_length() - 1 + cross))
-    wrow = wide // 2
-    piece = wrow // n
+    halves = 2 if heads % 2 == 0 and wide // 2 // n >= 16 else 1
+    hw = wide // halves
+    cols = width // 2
     pieces = n - 1
     vm = pltpu.VMEM
     dma = pltpu.SemaphoreType.DMA
@@ -465,26 +531,27 @@
         vm((2, LEAF, 2 * wide), BF16),
         vm((2, LEAF, 2 * wide), BF16),
         vm((coarse, wide), F32),
-        vm((wide, width), F32),
-        vm((wrow, width), BF16),
-        vm((wrow, width), BF16),
-        vm((wrow, width), BF16),
-        vm((pieces, piece, width), BF16),
-        vm((2, wrow, width), BF16),
-        dma((2,)), dma((2,)),
-        dma((pieces,)), dma((pieces,)),
-        dma((pieces,)), dma((pieces,)),
-        dma((2,)), dma((2,)),
-        dma, dma,
-        dma((pieces,)), dma((pieces,)),
-        dma((pieces,)), dma((pieces,)),
-        dma, dma,
+        vm((halves, hw, width), F32),
+        vm((halves, hw, cols), BF16),
+        vm((halves, hw, cols), BF16),
+        vm((halves, hw, cols), F32),
+        vm((halves, hw, cols), BF16),
+        vm((halves, hw, cols), BF16),
+        vm((halves, 2, hw, cols), BF16),
+        dma((halves, 2)), dma((halves, 2)),
+        dma((halves, pieces)), dma((halves, pieces)),
+        dma((halves, pieces)), dma((halves, pieces)),
+        dma((halves, 2)), dma((halves, 2)),
+        dma((halves,)), dma((halves,)),
+        dma((halves, cross)), dma((halves, cross)),
+        dma((halves, cross)), dma((halves, cross)),
+        dma((halves,)), dma((halves,)),
     ]
     spec = pl.BlockSpec(memory_space=pltpu.VMEM)
     out = pl.pallas_call(
-        functools.partial(kernel, n, heads, rows),
+        functools.partial(kernel, n, heads, rows, halves),
         out_shape=[jax.ShapeDtypeStruct((rows, wide), BF16)] * 3
-        + [jax.ShapeDtypeStruct((wide, width), F32)],
+        + [jax.ShapeDtypeStruct((halves, 2, hw, cols), BF16)],
         in_specs=[spec] * 5,
         out_specs=[spec] * 4,
         scratch_shapes=scratch,
@@ -492,7 +559,14 @@
             collective_id=0, has_side_effects=True, vmem_limit_bytes=56 * 2**20
         ),
     )(queries[0], key_states[0], value_states[0], grad_out[0], out_weight)
-    return out[0][None], out[1][None], out[2][None], out[3]
+    small = jax.ShapeDtypeStruct((rows, wide), BF16)
+    dq, dk, dv, gw = pl.pallas_call(
+        settle,
+        out_shape=[small, small, small, jax.ShapeDtypeStruct((wide, width), F32)],
+        in_specs=[spec] * 4,
+        out_specs=[spec] * 4,
+    )(*out)
+    return dq[None], dk[None], dv[None], gw
 
 
 def solution(mesh):

time: 87 us -> 75.7 us (0.87)
  local copies, waits for them, and re-layouts: 7.07 us -> 0 us
  Pallas kernels: 79 us -> 74.9 us
    unnamed x6 -> x0, local copies, waits for them, and re-layouts: 7.07 us -> none
    pallas_call x1 -> x2, Pallas kernels: 79 us -> 74.9 us  [the longest x1 71.3 us: body(): pl.pallas_call(functools.partial(kernel, n, heads, rows, halves), out_sha...]
where the time goes in v1:
time: 75.7 us; the launch traced here: 75.5 us
  Pallas kernels  74.9 us (99%)
    pallas_call x1, Pallas kernels, body(): pl.pallas_call(functools.partial(kernel, n, heads, rows, halves), out_sha...  71.3 us
    pallas_call x1, Pallas kernels, body(): pl.pallas_call(settle, out_shape=[small, small, small, jax.ShapeDtypeStru...  3.58 us

profile of v1, /device:TPU:0, one launch (start us, length us, event | category | flops | bytes accessed | tf_op | source)
XLA Modules:
  0.0 75.5 jit_solution(13235257823204342508)
XLA Ops:
  0.6 71.3 %shard_map.84 = (bf16[512,512]{1,0:T(8,128)(2,1)}, bf16[512,512]{1,0:T(8,128)(2,1)}, bf16[512,512]{1,0:T(8,128)(2,1)}, bf16[2,2,256,512]{3,2,1,0:T(8,128)(2,1)}) custom-call(bf16[512,512]{1,0:T(8,128)(2,1)} %bitcast.8, bf16[512,512]{1,0:T(8,128)(2,1)} %bitcast.9, bf16[512,512]{1,0:T(8,128)(2,1)} %bitcast.10, bf16[512,1024]{1,0:T(8,128)(2,1)} %bitcast.7, ...), custom_call_target="tpu_custom_call" | custom-call | tf_op jit(solution)/shard_map/pallas_call | solution.py:551
  71.9 3.6 %shard_map.85 = (bf16[512,512]{1,0:T(8,128)(2,1)}, bf16[512,512]{1,0:T(8,128)(2,1)}, bf16[512,512]{1,0:T(8,128)(2,1)}, f32[512,1024]{1,0:T(8,128)}) custom-call(bf16[512,512]{1,0:T(8,128)(2,1)} %get-tuple-element.12.dq_in, bf16[512,512]{1,0:T(8,128)(2,1)} %get-tuple-element.13.dk_in, bf16[512,512]{1,0:T(8,128)(2,1)} %get-tuple-element.14.dv_in, ...), custom_call_target="tpu_custom_call" | custom-call | tf_op jit(solution)/shard_map/pallas_call | solution.py:563

commit v2 on v1

--- a/solution.py
+++ b/solution.py
@@ -178,7 +178,8 @@
             for c in sib_copies(u, b):
                 c.wait_send()
 
-    send_kv(0)
+    for u in range(halves):
+        send_kv(u)
 
     for b in range(blocks // 2):
         ql[b * LEAF : (b + 1) * LEAF] = pool(q_ref[2 * b * LEAF : 2 * (b + 1) * LEAF], LEAF)
@@ -281,12 +282,8 @@
         return carry
 
     half_cols = go_ref.shape[1] // 2
-    steps = cross
     my_cols = pl.ds(pl.multiple_of(core * half_cols, half_cols), half_cols)
     other_cols = pl.ds(pl.multiple_of(other * half_cols, half_cols), half_cols)
-
-    def bit(s):
-        return lax.rem(ctx // (1 << s), 2)
 
     def weight_grad(u):
         for b in range(per):
@@ -297,32 +294,35 @@
         yield
         pair.wait()
         wacc[u] = wpart[u, :, my_cols] + wrecv[u].astype(F32)
-        lo, size, got = 0, hw, 0
-        for s in range(steps):
-            size //= 2
-            give = pl.multiple_of(lo + (1 - bit(s)) * size, size)
-            lo = lo + bit(s) * size
-            keep = pl.multiple_of(lo, size)
-            wtx[u, pl.ds(give, size)] = wacc[u, pl.ds(give, size)].astype(BF16)
-            c = remote(wtx.at[u, pl.ds(give, size)], wrx.at[u, pl.ds(got, size)],
-                       rs_s.at[u, s], rs_r.at[u, s], ctx=ctx ^ (1 << s))
+        piece = hw // n
+        wtx[u] = wacc[u].astype(BF16)
+        mine = pl.ds(pl.multiple_of(ctx * piece, piece), piece)
+
+        def part(m):
+            return pl.ds(pl.multiple_of((ctx ^ m) * piece, piece), piece)
+
+        out = []
+        for m in range(1, n):
+            c = remote(wtx.at[u, part(m)], wrx.at[u, pl.ds((m - 1) * piece, piece)],
+                       rs_s.at[u, m - 1], rs_r.at[u, m - 1], ctx=ctx ^ m)
             c.start()
-            yield
-            c.wait()
-            wacc[u, pl.ds(keep, size)] += wrx[u, pl.ds(got, size)].astype(F32)
-            got += size
-        wfin[u, core, pl.ds(pl.multiple_of(lo, size), size)] = wacc[u, pl.ds(pl.multiple_of(lo, size), size)].astype(BF16)
-        for s in reversed(range(steps)):
-            mine = pl.ds(pl.multiple_of(lo, size), size)
-            theirs = pl.ds(pl.multiple_of(lo + (1 - 2 * bit(s)) * size, size), size)
-            peer = ctx ^ (1 << s)
-            c = remote(wfin.at[u, core, mine], wfin.at[u, core, mine], ag_s.at[u, s], ag_r.at[u, s], ctx=peer)
+            out.append(c)
+        yield
+        tot = wacc[u, mine]
+        for m in range(1, n):
+            out[m - 1].wait()
+            tot = tot + wrx[u, (m - 1) * piece : m * piece].astype(F32)
+        wfin[u, core, mine] = tot.astype(BF16)
+        out = []
+        for m in range(1, n):
+            c = remote(wfin.at[u, core, mine], wfin.at[u, core, mine], ag_s.at[u, m - 1], ag_r.at[u, m - 1], ctx=ctx ^ m)
             c.start()
-            yield
-            c.wait_send()
-            remote(wfin.at[u, core, mine], wfin.at[u, core, theirs], ag_s.at[u, s], ag_r.at[u, s], ctx=peer).wait_recv()
-            lo = lo - bit(s) * size
-            size *= 2
+            out.append(c)
+        yield
+        for m in range(1, n):
+            out[m - 1].wait_send()
+            remote(wfin.at[u, core, mine], wfin.at[u, core, part(m)], ag_s.at[u, m - 1], ag_r.at[u, m - 1],
+                   ctx=ctx ^ m).wait_recv()
         c = remote(wfin.at[u, core], wfin.at[u, core], wf_s.at[u], wf_r.at[u], batch=other)
         c.start()
         yield
@@ -459,14 +459,14 @@
 
     for u in range(halves):
         take_kv(u)
-        if u + 1 < halves:
-            send_kv(u + 1)
         lax.fori_loop(u * per, (u + 1) * per, forward, 0)
+        advance()
         chains.append(weight_grad(u))
-        advance()
+        next(chains[-1])
         lax.fori_loop(u * per, (u + 1) * per, back_cross, 0)
         send_grads(u)
         advance()
+    for u in range(halves):
         lax.fori_loop(u * per, (u + 1) * per, back_level0, 0)
         send_rims(u)
         advance()
@@ -543,8 +543,8 @@
         dma((halves, pieces)), dma((halves, pieces)),
         dma((halves, 2)), dma((halves, 2)),
         dma((halves,)), dma((halves,)),
-        dma((halves, cross)), dma((halves, cross)),
-        dma((halves, cross)), dma((halves, cross)),
+        dma((halves, pieces)), dma((halves, pieces)),
+        dma((halves, pieces)), dma((halves, pieces)),
         dma((halves,)), dma((halves,)),
     ]
     spec = pl.BlockSpec(memory_space=pltpu.VMEM)

time: 75.7 us -> 71.8 us (0.948)
  Pallas kernels: 74.9 us -> 71 us
    pallas_call x1, Pallas kernels: 71.3 us -> 67.4 us  [body(): pl.pallas_call(functools.partial(kernel, n, heads, rows, halves), out_sha...]
where the time goes in v2:
time: 71.8 us; the launch traced here: 71.6 us
  Pallas kernels  71 us (99%)
    pallas_call x1, Pallas kernels, body(): pl.pallas_call(functools.partial(kernel, n, heads, rows, halves), out_sha...  67.4 us
    pallas_call x1, Pallas kernels, body(): pl.pallas_call(settle, out_shape=[small, small, small, jax.ShapeDtypeStru...  3.58 us

profile of v2, /device:TPU:0, one launch (start us, length us, event | category | flops | bytes accessed | tf_op | source)
XLA Modules:
  0.0 71.6 jit_solution(13049363242322120786)
XLA Ops:
  0.6 67.4 %shard_map.84 = (bf16[512,512]{1,0:T(8,128)(2,1)}, bf16[512,512]{1,0:T(8,128)(2,1)}, bf16[512,512]{1,0:T(8,128)(2,1)}, bf16[2,2,256,512]{3,2,1,0:T(8,128)(2,1)}) custom-call(bf16[512,512]{1,0:T(8,128)(2,1)} %bitcast.8, bf16[512,512]{1,0:T(8,128)(2,1)} %bitcast.9, bf16[512,512]{1,0:T(8,128)(2,1)} %bitcast.10, bf16[512,1024]{1,0:T(8,128)(2,1)} %bitcast.7, ...), custom_call_target="tpu_custom_call" | custom-call | tf_op jit(solution)/shard_map/pallas_call | solution.py:551
  68.0 3.6 %shard_map.85 = (bf16[512,512]{1,0:T(8,128)(2,1)}, bf16[512,512]{1,0:T(8,128)(2,1)}, bf16[512,512]{1,0:T(8,128)(2,1)}, f32[512,1024]{1,0:T(8,128)}) custom-call(bf16[512,512]{1,0:T(8,128)(2,1)} %get-tuple-element.12.dq_in, bf16[512,512]{1,0:T(8,128)(2,1)} %get-tuple-element.13.dk_in, bf16[512,512]{1,0:T(8,128)(2,1)} %get-tuple-element.14.dv_in, ...), custom_call_target="tpu_custom_call" | custom-call | tf_op jit(solution)/shard_map/pallas_call | solution.py:563
